TPU v7x, 32 devices: a whole 2x2x4 slice. The times are simulated.
32 devices in a mesh: lat: 4 (over x, core), lon: 4 (over z), lev: 2 (over y).
Axes of the slice: x: 2, y: 2, z: 4, core: 2. Of those that a mesh axis runs over, the one named last changes fastest.
Arguments:
- gradient: float32 [132, 128, 1536], P('lev', 'lat', 'lon'), may hold values from -6 to 6
- vertical: float32 [132, 132], replicated, may hold values from -0.5 to 0.5
- variance: float32 [132, 128, 1536], P('lev', 'lat', 'lon'), may hold values from 0.25 to 4
Outputs:
- increment: float32 [132, 128, 1536], P('lev', 'lat', 'lon')
All inputs are finite; a program needn't handle non-finite values.
Results may differ from a plain program's by a relative error of at most 0.000078.
Values sent between devices are 32-bit elements; how exact they have to be, the bound alone decides.
A program may use at most 64 MiB of HBM per device.

v0:
```python
import functools
import math

import jax
import jax.numpy as jnp
import ml_dtypes
import numpy as np
from jax import lax
from jax.experimental import pallas as pl
from jax.experimental.pallas import tpu as pltpu
from jax.sharding import PartitionSpec as P

HALO = 32
MAX_CHUNKS = 11
AHEAD = 2
LANES = 128
MESH = pl.DeviceIdType.MESH


def taps(offset):
    steps = np.arange(-HALO, HALO + 1, dtype=np.float64)
    bell = np.exp(-0.5 * (2.0 * steps / HALO) ** 2)
    scale = 1.0 / (math.sqrt(bell.sum()) * math.sqrt(math.sqrt((bell * bell).sum())))
    values = np.exp(-0.5 * (2.0 * offset / HALO) ** 2) * scale
    return np.where(np.abs(offset) <= HALO, values, 0.0).astype(np.float32)


def parts_np(values):
    high = values.astype(ml_dtypes.bfloat16)
    low = (values - high.astype(np.float32)).astype(ml_dtypes.bfloat16)
    return high, low


def lat_matrix(rows):
    place = np.arange(-HALO, rows + HALO)
    high, low = parts_np(taps((place[None, :] - np.arange(rows)[:, None]).astype(np.float64)))
    return np.concatenate(
        [np.concatenate([high, high], 1), np.concatenate([low, np.zeros_like(low)], 1)], 0
    )


def lon_matrices(cols):
    place = np.concatenate([np.arange(cols), np.arange(-HALO, 0), np.arange(cols, cols + HALO)])
    values = taps((place[:, None] - np.arange(cols)[None, :]).astype(np.float64))
    values = np.pad(values, ((0, LANES - 2 * HALO), (0, 0)))
    return np.stack(parts_np(values))


def split(x):
    high = x.astype(jnp.bfloat16)
    return high, (x - high.astype(jnp.float32)).astype(jnp.bfloat16)


def dot(a, b):
    return jnp.dot(a, b, preferred_element_type=jnp.float32)


def kernel(
    sizes, g_hbm, v_ref, var_hbm, plat_ref, qlon_hbm, out_hbm,
    g, part, own, ry, col, hx1, pc, ez1, rz1, sc, ez2, rz2, q2, hx2, out, var, qlon,
    in_sem, ys, yr, x1s, x1r, z1s, z1r, z2s, z2r, x2s, x2r, out_sem,
):
    levels, rows, cols, n_lev, n_lat, n_lon, chunks, padded = sizes
    each = levels // chunks
    span = each * rows
    groups = LANES // HALO
    band = rows // groups
    espan = each * band

    lev, lat, lon = lax.axis_index("lev"), lax.axis_index("lat"), lax.axis_index("lon")
    lon_next, lon_prev = lax.rem(lon + 1, n_lon), lax.rem(lon + n_lon - 1, n_lon)
    has_prev, has_next = lat > 0, lat < n_lat - 1

    tiles = cols // LANES
    loads_g = [
        pltpu.make_async_copy(
            g_hbm.at[:, pl.ds(c * LANES, LANES)], g.at[c, pl.ds(0, levels * rows)], in_sem.at[2 + c]
        )
        for c in range(tiles)
    ]
    load_q = pltpu.make_async_copy(qlon_hbm, qlon, in_sem.at[1])
    load_v = pltpu.make_async_copy(var_hbm, var, in_sem.at[0])
    for load in loads_g:
        load.start()
    load_q.start()
    load_v.start()

    barrier = pltpu.get_barrier_semaphore()

    def greet(target):
        pl.semaphore_signal(barrier, inc=1, device_id=target, device_id_type=MESH)

    for d in range(1, n_lev):
        greet({"lev": lax.rem(lev + d, n_lev)})
    greet({"lon": lon_next})
    greet({"lon": lon_prev})

    @pl.when(has_prev)
    def _():
        greet({"lat": lat - 1})

    @pl.when(has_next)
    def _():
        greet({"lat": lat + 1})

    peers = n_lev + 1 + jnp.minimum(lat, 1) + jnp.minimum(n_lat - 1 - lat, 1)
    pl.semaphore_wait(barrier, peers)

    if padded > levels:
        g[:, levels * rows:, :] = jnp.zeros((tiles, (padded - levels) * rows, LANES), jnp.float32)
    for load in loads_g:
        load.wait()

    def mixing(owner):
        block = jnp.zeros((levels, levels), jnp.float32)
        for a in range(n_lev):
            for b in range(n_lev):
                piece = v_ref[a * levels:(a + 1) * levels, b * levels:(b + 1) * levels]
                block = jnp.where(jnp.logical_and(owner == a, lev == b), piece, block)
        block = jnp.concatenate([block, jnp.zeros((levels, padded - levels), jnp.float32)], axis=1)
        high, low = split(block)
        return jnp.concatenate([high, low, high], axis=1)

    def mix(matrix, store):
        def body(r, carry):
            x = jnp.concatenate([g[c, pl.ds(r, padded, stride=rows), :] for c in range(tiles)], axis=1)
            high, low = split(x)
            store(r, dot(matrix, jnp.concatenate([high, high, low], axis=0)))
            return carry

        lax.fori_loop(0, rows, body, 0, unroll=2)

    def y_copy(d, k):
        at = pl.ds(pl.multiple_of(k * span, span), span)
        return pltpu.make_async_remote_copy(
            part.at[d - 1, :, at], ry.at[d - 1, :, at], ys.at[d - 1, k], yr.at[d - 1, k],
            device_id={"lev": lax.rem(lev + d, n_lev)}, device_id_type=MESH,
        )

    def x_copy(src, dst, send, recv, side, k):
        at = pl.ds(pl.multiple_of(k * span, span), span)
        return pltpu.make_async_remote_copy(
            src.at[at], dst.at[side, at], send.at[side, k], recv.at[side, k],
            device_id={"lat": jnp.clip(lat + (1 if side == 0 else -1), 0, n_lat - 1)}, device_id_type=MESH,
        )

    def z_copy(src, dst, send, recv, side, k):
        at = pl.ds(pl.multiple_of(k * espan, espan), espan)
        return pltpu.make_async_remote_copy(
            src.at[side, at], dst.at[side, at], send.at[side, k], recv.at[side, k],
            device_id={"lon": lon_next if side == 0 else lon_prev}, device_id_type=MESH,
        )

    def x_send(*a, k):
        @pl.when(has_next)
        def _():
            x_copy(*a, 0, k).start()

        @pl.when(has_prev)
        def _():
            x_copy(*a, 1, k).start()

    def x_recv(*a, k):
        @pl.when(has_prev)
        def _():
            x_copy(*a, 0, k).wait_recv()

        @pl.when(has_next)
        def _():
            x_copy(*a, 1, k).wait_recv()

    lane = lax.broadcasted_iota(jnp.int32, (espan, LANES), 1)

    def pack(tile, base):
        tile = tile.reshape(each, groups, band, LANES)
        packed = None
        for q in range(groups):
            shift = (HALO * q - base) % LANES
            moved = tile[:, q].reshape(espan, LANES)
            moved = pltpu.roll(moved, shift, 1) if shift else moved
            packed = moved if packed is None else jnp.where(lane >= HALO * q, moved, packed)
        return packed

    def unpack(left, right):
        out_rows = []
        for q in range(groups):
            a, b = (-HALO * q) % LANES, (HALO - HALO * q) % LANES
            moved_l = pltpu.roll(left, a, 1) if a else left
            moved_r = pltpu.roll(right, b, 1) if b else right
            out_rows.append(jnp.where(lane < HALO, moved_l, moved_r).reshape(each, 1, band, LANES))
        return jnp.concatenate(out_rows, axis=1).reshape(span, LANES)

    def along_lat(before, here, after):
        blocks = jnp.concatenate(
            [
                jnp.concatenate([x[i * rows:(i + 1) * rows] for i in range(each)], axis=1)
                for x in (before, here, after)
            ],
            axis=0,
        )
        high, low = split(blocks)
        both = dot(plat_ref[...], jnp.concatenate([high, low], axis=0))
        both = both[:rows] + both[rows:]
        return jnp.concatenate([both[:, i * cols:(i + 1) * cols] for i in range(each)], axis=0)

    def along_lon(here, left, right):
        high, low = split(jnp.concatenate([here, unpack(left, right)], axis=1))
        return dot(high, qlon[0]) + (dot(low, qlon[0]) + dot(high, qlon[1]))

    for d in range(1, n_lev):
        def store(r, value, d=d):
            for c in range(tiles):
                part[d - 1, c, pl.ds(r, levels, stride=rows), :] = value[:, c * LANES:(c + 1) * LANES]

        mix(mixing(lax.rem(lev + d, n_lev)), store)
    for k in range(min(AHEAD, chunks)):
        for d in range(1, n_lev):
            y_copy(d, k).start()

    def store_own(r, value):
        for c in range(tiles):
            own[c, pl.ds(r, levels, stride=rows), :] = value[:, c * LANES:(c + 1) * LANES]

    mix(mixing(lev), store_own)

    @pl.when(jnp.logical_not(has_prev))
    def _():
        hx1[0] = jnp.zeros((levels * rows, cols), jnp.float32)
        hx2[0] = jnp.zeros((levels * rows, cols), jnp.float32)

    @pl.when(jnp.logical_not(has_next))
    def _():
        hx1[1] = jnp.zeros((levels * rows, cols), jnp.float32)
        hx2[1] = jnp.zeros((levels * rows, cols), jnp.float32)

    load_q.wait()
    load_v.wait()

    x1 = (col, hx1, x1s, x1r)
    x2 = (q2, hx2, x2s, x2r)
    z1 = (ez1, rz1, z1s, z1r)
    z2 = (ez2, rz2, z2s, z2r)

    def out_copy(k):
        at = pl.ds(pl.multiple_of(k * span, span), span)
        return pltpu.make_async_copy(out.at[at], out_hbm.at[at], out_sem.at[k])

    def z_send(value, edges, args, k):
        eat = pl.ds(pl.multiple_of(k * espan, espan), espan)
        edges[0, eat] = pack(value[:, cols - LANES:], LANES - HALO)
        edges[1, eat] = pack(value[:, :LANES], 0)
        z_copy(*args, 0, k).start()
        z_copy(*args, 1, k).start()

    def z_recv(recv, args, k):
        z_copy(*args, 0, k).wait_recv()
        z_copy(*args, 1, k).wait_recv()
        eat = pl.ds(pl.multiple_of(k * espan, espan), espan)
        return recv[0, eat], recv[1, eat]

    def step(t, carry):
        def stage(lag, body):
            k = t - lag

            @pl.when(jnp.logical_and(k >= 0, k < chunks))
            def _():
                body(k, pl.ds(pl.multiple_of(k * span, span), span))

        def stage_send(k, at):
            for d in range(1, n_lev):
                y_copy(d, k).start()

        def stage_mix(k, at):
            total = own[:, at]
            for d in range(1, n_lev):
                y_copy(d, k).wait_recv()
                total = total + ry[d - 1, :, at]
            for c in range(tiles):
                col[at, c * LANES:(c + 1) * LANES] = total[c]
            x_send(*x1, k=k)

        def stage_p1(k, at):
            x_recv(*x1, k=k)
            value = along_lat(hx1[0, at], col[at], hx1[1, at])
            pc[at] = value
            z_send(value, ez1, z1, k)

        def stage_q1(k, at):
            left, right = z_recv(rz1, z1, k)
            value = var[at] * along_lon(pc[at], left, right)
            sc[at] = value
            z_send(value, ez2, z2, k)

        def stage_q2(k, at):
            left, right = z_recv(rz2, z2, k)
            q2[at] = along_lon(sc[at], left, right)
            x_send(*x2, k=k)

        def stage_p2(k, at):
            x_recv(*x2, k=k)
            out[at] = along_lat(hx2[0, at], q2[at], hx2[1, at])
            out_copy(k).start()

        stage(-AHEAD, stage_send)
        stage(0, stage_mix)
        stage(1, stage_p1)
        stage(2, stage_q1)
        stage(3, stage_q2)
        stage(4, stage_p2)
        return carry

    lax.fori_loop(0, chunks + 4, step, 0)

    def drain(k, carry):
        for d in range(1, n_lev):
            y_copy(d, k).wait_send()
        for args in (z1, z2):
            z_copy(*args, 0, k).wait_send()
            z_copy(*args, 1, k).wait_send()

        @pl.when(has_next)
        def _():
            x_copy(*x1, 0, k).wait_send()
            x_copy(*x2, 0, k).wait_send()

        @pl.when(has_prev)
        def _():
            x_copy(*x1, 1, k).wait_send()
            x_copy(*x2, 1, k).wait_send()

        out_copy(k).wait()
        return carry

    lax.fori_loop(0, chunks, drain, 0)


def on_device(gradient, vertical, variance):
    levels, rows, cols = gradient.shape
    n_lev, n_lat, n_lon = (lax.axis_size(a) for a in ("lev", "lat", "lon"))
    chunks = max(c for c in range(1, MAX_CHUNKS + 1) if levels % c == 0)
    padded = -(-levels // 16) * 16
    band = rows * HALO // LANES
    sizes = (levels, rows, cols, n_lev, n_lat, n_lon, chunks, padded)
    plane = levels * rows
    f32 = jnp.float32
    dma = pltpu.SemaphoreType.DMA
    qlon = lon_matrices(cols)
    plat = lat_matrix(rows)
    anywhere = pl.BlockSpec(memory_space=pl.ANY)
    vmem = pl.BlockSpec(memory_space=pltpu.VMEM)
    full = pltpu.VMEM((plane, cols), f32)
    tiles = cols // LANES
    others = pltpu.VMEM((n_lev - 1, tiles, plane, LANES), f32)
    own = pltpu.VMEM((tiles, plane, LANES), f32)
    sides = pltpu.VMEM((2, plane, cols), f32)
    edges = pltpu.VMEM((2, levels * band, LANES), f32)
    pair = dma((2, chunks))
    result = pl.pallas_call(
        functools.partial(kernel, sizes),
        out_shape=jax.ShapeDtypeStruct((plane, cols), f32),
        in_specs=[anywhere, vmem, anywhere, vmem, anywhere],
        out_specs=anywhere,
        scratch_shapes=[
            pltpu.VMEM((tiles, padded * rows, LANES), f32),
            others, own, others, full, sides, full, edges, edges, full, edges, edges, full, sides, full, full,
            pltpu.VMEM(qlon.shape, jnp.bfloat16),
            dma((2 + tiles,)), dma((n_lev - 1, chunks)), dma((n_lev - 1, chunks)),
            pair, pair, pair, pair, pair, pair, pair, pair, dma((chunks,)),
        ],
        compiler_params=pltpu.CompilerParams(
            collective_id=0, has_side_effects=True, vmem_limit_bytes=60 * 1024 * 1024
        ),
    )(
        gradient.reshape(plane, cols), vertical, variance.reshape(plane, cols),
        jnp.asarray(plat), jnp.asarray(qlon),
    )
    return result.reshape(levels, rows, cols)


def solution(mesh):
    return jax.shard_map(
        on_device,
        mesh=mesh,
        in_specs=(P("lev", "lat", "lon"), P(), P("lev", "lat", "lon")),
        out_specs=P("lev", "lat", "lon"),
        check_vma=False,
    )
```

profile of v0, /device:TPU:1, one launch (start us, length us, event | category | flops | bytes accessed | tf_op | source)
XLA Modules:
  0.0 112.8 jit_solution(2688941210543421907)
XLA Ops:
  0.0 108.9 %shard_map.55 = f32[2112,384]{1,0:T(8,128)} custom-call(f32[2112,384]{1,0:T(8,128)} %bitcast.4, f32[132,132]{1,0:T(8,128)} %v_ref.1, f32[2112,384]{1,0:T(8,128)} %bitcast.5, bf16[64,192]{1,0:T(8,128)(2,1)} %constant.4.clone.plat_ref, bf16[2,512,384]{2,1,0:T(8,128)(2,1)} %constant.5.clone.qlon_hbm), custom_call_target="tpu_custom_call" | custom-call | tf_op jit(solution)/shard_map/pallas_call | solution.py:358
  108.9 3.8 %copy.7 = f32[66,32,384]{2,1,0:T(8,128)} copy(f32[66,32,384]{2,1,0:T(8,128)} %bitcast.3) | data formatting | bytes 6488064
where the time goes:
time: 113 us
  Pallas kernels  109 us (96%)
  local copies, waits for them, and re-layouts  3.83 us (3%)
    pallas_call x1, Pallas kernels, on_device(): pl.pallas_call(functools.partial(kernel, sizes), out_shape=jax.ShapeDtype...  109 us
    unnamed x1, local copies, waits for them, and re-layouts  3.83 us

commit v1 on v0

--- a/solution.py
+++ b/solution.py
@@ -12,7 +12,7 @@
 
 HALO = 32
 MAX_CHUNKS = 11
-AHEAD = 2
+AHEAD = 4
 LANES = 128
 MESH = pl.DeviceIdType.MESH
 
@@ -57,8 +57,8 @@
 
 def kernel(
     sizes, g_hbm, v_ref, var_hbm, plat_ref, qlon_hbm, out_hbm,
-    g, part, own, ry, col, hx1, pc, ez1, rz1, sc, ez2, rz2, q2, hx2, out, var, qlon,
-    in_sem, ys, yr, x1s, x1r, z1s, z1r, z2s, z2r, x2s, x2r, out_sem,
+    g, hg, pg, part, own, ry, col, hx1, pc, ez1, rz1, sc, ez2, rz2, q2, hx2, out, var, qlon,
+    in_sem, xgs, xgr, ys, yr, x1s, x1r, z1s, z1r, z2s, z2r, x2s, x2r, out_sem,
 ):
     levels, rows, cols, n_lev, n_lat, n_lon, chunks, padded = sizes
     each = levels // chunks
@@ -72,6 +72,9 @@
     has_prev, has_next = lat > 0, lat < n_lat - 1
 
     tiles = cols // LANES
+    last = tiles - 1
+    main = cols - LANES
+    plane = levels * rows
     loads_g = [
         pltpu.make_async_copy(
             g_hbm.at[:, pl.ds(c * LANES, LANES)], g.at[c, pl.ds(0, levels * rows)], in_sem.at[2 + c]
@@ -80,7 +83,7 @@
     ]
     load_q = pltpu.make_async_copy(qlon_hbm, qlon, in_sem.at[1])
     load_v = pltpu.make_async_copy(var_hbm, var, in_sem.at[0])
-    for load in loads_g:
+    for load in loads_g[::-1]:
         load.start()
     load_q.start()
     load_v.start()
@@ -106,9 +109,27 @@
     peers = n_lev + 1 + jnp.minimum(lat, 1) + jnp.minimum(n_lat - 1 - lat, 1)
     pl.semaphore_wait(barrier, peers)
 
+    loads_g[last].wait()
+
+    def raw_copy(side):
+        return pltpu.make_async_remote_copy(
+            g.at[last, pl.ds(0, plane)], hg.at[side], xgs.at[side], xgr.at[side],
+            device_id={"lat": jnp.clip(lat + (1 if side == 0 else -1), 0, n_lat - 1)}, device_id_type=MESH,
+        )
+
+    @pl.when(has_next)
+    def _():
+        raw_copy(0).start()
+
+    @pl.when(has_prev)
+    def _():
+        raw_copy(1).start()
+
     if padded > levels:
-        g[:, levels * rows:, :] = jnp.zeros((tiles, (padded - levels) * rows, LANES), jnp.float32)
-    for load in loads_g:
+        extra = (padded - levels) * rows
+        g[:last, plane:, :] = jnp.zeros((last, extra, LANES), jnp.float32)
+        pg[plane:, :] = jnp.zeros((extra, LANES), jnp.float32)
+    for load in loads_g[:last]:
         load.wait()
 
     def mixing(owner):
@@ -121,19 +142,37 @@
         high, low = split(block)
         return jnp.concatenate([high, low, high], axis=1)
 
-    def mix(matrix, store):
+    def mix(matrix, wanted, store):
         def body(r, carry):
-            x = jnp.concatenate([g[c, pl.ds(r, padded, stride=rows), :] for c in range(tiles)], axis=1)
+            at = pl.ds(r, padded, stride=rows)
+            x = jnp.concatenate([pg[at, :] if c == last else g[c, at, :] for c in wanted], axis=1)
             high, low = split(x)
-            store(r, dot(matrix, jnp.concatenate([high, high, low], axis=0)))
+            value = dot(matrix, jnp.concatenate([high, high, low], axis=0))
+            for i, c in enumerate(wanted):
+                store(c, pl.ds(r, levels, stride=rows), value[:, i * LANES:(i + 1) * LANES])
             return carry
 
-        lax.fori_loop(0, rows, body, 0, unroll=2)
-
-    def y_copy(d, k):
+        lax.fori_loop(0, rows, body, 0, unroll=4)
+
+    def mix_others(wanted):
+        for d in range(1, n_lev):
+            def store(c, at, value, d=d):
+                part[d - 1, c, at, :] = value
+
+            mix(mixing(lax.rem(lev + d, n_lev)), wanted, store)
+
+    def mix_own(wanted):
+        def store(c, at, value):
+            own[c, at, :] = value
+
+        mix(mixing(lev), wanted, store)
+
+    def y_copy(d, k, late):
         at = pl.ds(pl.multiple_of(k * span, span), span)
+        which = pl.ds(last, 1) if late else pl.ds(0, last)
         return pltpu.make_async_remote_copy(
-            part.at[d - 1, :, at], ry.at[d - 1, :, at], ys.at[d - 1, k], yr.at[d - 1, k],
+            part.at[d - 1, which, at], ry.at[d - 1, which, at],
+            ys.at[d - 1, 2 * k + late], yr.at[d - 1, 2 * k + late],
             device_id={"lev": lax.rem(lev + d, n_lev)}, device_id_type=MESH,
         )
 
@@ -191,6 +230,7 @@
         return jnp.concatenate(out_rows, axis=1).reshape(span, LANES)
 
     def along_lat(before, here, after):
+        width = here.shape[1]
         blocks = jnp.concatenate(
             [
                 jnp.concatenate([x[i * rows:(i + 1) * rows] for i in range(each)], axis=1)
@@ -201,37 +241,49 @@
         high, low = split(blocks)
         both = dot(plat_ref[...], jnp.concatenate([high, low], axis=0))
         both = both[:rows] + both[rows:]
-        return jnp.concatenate([both[:, i * cols:(i + 1) * cols] for i in range(each)], axis=0)
+        return jnp.concatenate([both[:, i * width:(i + 1) * width] for i in range(each)], axis=0)
 
     def along_lon(here, left, right):
         high, low = split(jnp.concatenate([here, unpack(left, right)], axis=1))
         return dot(high, qlon[0]) + (dot(low, qlon[0]) + dot(high, qlon[1]))
 
-    for d in range(1, n_lev):
-        def store(r, value, d=d):
-            for c in range(tiles):
-                part[d - 1, c, pl.ds(r, levels, stride=rows), :] = value[:, c * LANES:(c + 1) * LANES]
-
-        mix(mixing(lax.rem(lev + d, n_lev)), store)
+    mix_others(range(last))
     for k in range(min(AHEAD, chunks)):
         for d in range(1, n_lev):
-            y_copy(d, k).start()
-
-    def store_own(r, value):
-        for c in range(tiles):
-            own[c, pl.ds(r, levels, stride=rows), :] = value[:, c * LANES:(c + 1) * LANES]
-
-    mix(mixing(lev), store_own)
+            y_copy(d, k, 0).start()
+    mix_own(range(last))
 
     @pl.when(jnp.logical_not(has_prev))
     def _():
-        hx1[0] = jnp.zeros((levels * rows, cols), jnp.float32)
+        hx1[0] = jnp.zeros((plane, main), jnp.float32)
+        hg[0] = jnp.zeros((plane, LANES), jnp.float32)
         hx2[0] = jnp.zeros((levels * rows, cols), jnp.float32)
 
     @pl.when(jnp.logical_not(has_next))
     def _():
-        hx1[1] = jnp.zeros((levels * rows, cols), jnp.float32)
+        hx1[1] = jnp.zeros((plane, main), jnp.float32)
+        hg[1] = jnp.zeros((plane, LANES), jnp.float32)
         hx2[1] = jnp.zeros((levels * rows, cols), jnp.float32)
+
+    @pl.when(has_prev)
+    def _():
+        raw_copy(0).wait_recv()
+
+    @pl.when(has_next)
+    def _():
+        raw_copy(1).wait_recv()
+
+    def early(k, carry):
+        at = pl.ds(pl.multiple_of(k * span, span), span)
+        pg[at] = along_lat(hg[0, at], g[last, at], hg[1, at])
+        return carry
+
+    lax.fori_loop(0, chunks, early, 0)
+    mix_others([last])
+    for k in range(min(AHEAD, chunks)):
+        for d in range(1, n_lev):
+            y_copy(d, k, 1).start()
+    mix_own([last])
 
     load_q.wait()
     load_v.wait()
@@ -267,21 +319,26 @@
                 body(k, pl.ds(pl.multiple_of(k * span, span), span))
 
         def stage_send(k, at):
+            for late in (0, 1):
+                for d in range(1, n_lev):
+                    y_copy(d, k, late).start()
+
+        def stage_mix(k, at):
+            total = own[:last, at]
             for d in range(1, n_lev):
-                y_copy(d, k).start()
-
-        def stage_mix(k, at):
-            total = own[:, at]
-            for d in range(1, n_lev):
-                y_copy(d, k).wait_recv()
-                total = total + ry[d - 1, :, at]
-            for c in range(tiles):
+                y_copy(d, k, 0).wait_recv()
+                total = total + ry[d - 1, :last, at]
+            for c in range(last):
                 col[at, c * LANES:(c + 1) * LANES] = total[c]
             x_send(*x1, k=k)
 
         def stage_p1(k, at):
             x_recv(*x1, k=k)
-            value = along_lat(hx1[0, at], col[at], hx1[1, at])
+            total = own[last, at]
+            for d in range(1, n_lev):
+                y_copy(d, k, 1).wait_recv()
+                total = total + ry[d - 1, last, at]
+            value = jnp.concatenate([along_lat(hx1[0, at], col[at], hx1[1, at]), total], axis=1)
             pc[at] = value
             z_send(value, ez1, z1, k)
 
@@ -313,7 +370,8 @@
 
     def drain(k, carry):
         for d in range(1, n_lev):
-            y_copy(d, k).wait_send()
+            y_copy(d, k, 0).wait_send()
+            y_copy(d, k, 1).wait_send()
         for args in (z1, z2):
             z_copy(*args, 0, k).wait_send()
             z_copy(*args, 1, k).wait_send()
@@ -332,6 +390,14 @@
         return carry
 
     lax.fori_loop(0, chunks, drain, 0)
+
+    @pl.when(has_next)
+    def _():
+        raw_copy(0).wait_send()
+
+    @pl.when(has_prev)
+    def _():
+        raw_copy(1).wait_send()
 
 
 def on_device(gradient, vertical, variance):
@@ -362,9 +428,11 @@
         out_specs=anywhere,
         scratch_shapes=[
             pltpu.VMEM((tiles, padded * rows, LANES), f32),
-            others, own, others, full, sides, full, edges, edges, full, edges, edges, full, sides, full, full,
+            pltpu.VMEM((2, plane, LANES), f32), pltpu.VMEM((padded * rows, LANES), f32),
+            others, own, others, pltpu.VMEM((plane, cols - LANES), f32),
+            pltpu.VMEM((2, plane, cols - LANES), f32), full, edges, edges, full, edges, edges, full, sides, full, full,
             pltpu.VMEM(qlon.shape, jnp.bfloat16),
-            dma((2 + tiles,)), dma((n_lev - 1, chunks)), dma((n_lev - 1, chunks)),
+            dma((2 + tiles,)), dma((2,)), dma((2,)), dma((n_lev - 1, 2 * chunks)), dma((n_lev - 1, 2 * chunks)),
             pair, pair, pair, pair, pair, pair, pair, pair, dma((chunks,)),
         ],
         compiler_params=pltpu.CompilerParams(

time: 113 us -> 106 us (0.938)
  Pallas kernels: 109 us -> 102 us
    pallas_call x1, Pallas kernels: 109 us -> 102 us  [on_device(): pl.pallas_call(functools.partial(kernel, sizes), out_shape=jax.ShapeDtype...]
where the time goes in v1:
time: 106 us; the launch traced here: 105 us
  Pallas kernels  102 us (96%)
  local copies, waits for them, and re-layouts  3.83 us (4%)
    pallas_call x1, Pallas kernels, on_device(): pl.pallas_call(functools.partial(kernel, sizes), out_shape=jax.ShapeDtype...  102 us
    unnamed x1, local copies, waits for them, and re-layouts  3.83 us

profile of v1, /device:TPU:1, one launch (start us, length us, event | category | flops | bytes accessed | tf_op | source)
XLA Modules:
  0.0 105.5 jit_solution(7713501692541263463)
XLA Ops:
  0.0 101.6 %shard_map.55 = f32[2112,384]{1,0:T(8,128)} custom-call(f32[2112,384]{1,0:T(8,128)} %bitcast.4, f32[132,132]{1,0:T(8,128)} %v_ref.1, f32[2112,384]{1,0:T(8,128)} %bitcast.5, bf16[64,192]{1,0:T(8,128)(2,1)} %constant.4.clone.plat_ref, bf16[2,512,384]{2,1,0:T(8,128)(2,1)} %constant.5.clone.qlon_hbm), custom_call_target="tpu_custom_call" | custom-call | tf_op jit(solution)/shard_map/pallas_call | solution.py:424
  101.6 3.8 %copy.7 = f32[66,32,384]{2,1,0:T(8,128)} copy(f32[66,32,384]{2,1,0:T(8,128)} %bitcast.3) | data formatting | bytes 6488064
